TPU v7x, 512 devices: a whole 4x4x16 slice. The times are simulated.
512 devices in a mesh: yz: 128 (over z_lo, x, y, core), gx: 4 (over z_hi).
Axes of the slice: x: 4, y: 4, z: 16 (z_hi: 4, z_lo: 4; z = z_hi * 4 + z_lo), core: 2. Of those that a mesh axis runs over, the one named last changes fastest.
Arguments:
- state: float32 [7, 64, 1024, 128], P(None, 'gx', 'yz'), may hold values from -2.5 to 2.5
- register: float32 [7, 64, 1024, 128], P(None, 'gx', 'yz'), may hold values from -3 to 3
- forcing: float32 [3, 64, 1024, 128], P(None, 'gx', 'yz'), may hold values from -3 to 3
- y_shift: int32 [1], replicated, may hold values from 0 to 1023
Outputs:
- new_state: float32 [7, 64, 1024, 128], P(None, 'gx', 'yz')
- new_register: float32 [7, 64, 1024, 128], P(None, 'gx', 'yz')
All inputs are finite; a program needn't handle non-finite values.
Results may differ from a plain program's by a relative error of at most 0.000092.
Values sent between devices are 32-bit elements; how exact they have to be, the bound alone decides.
A program may use at most 64 MiB of HBM per device.

v0:
```python
import jax
import jax.numpy as jnp
from jax import lax
from jax.sharding import PartitionSpec as P


def padded_2(block, sides, width):
    for axis, dim in sides:
        count = lax.axis_size(axis)
        forward = [(i, i + 1) for i in range(count - 1)]
        forward.append((count - 1, 0))
        backward = [(target, source) for source, target in forward]
        low = lax.ppermute(
            lax.slice_in_dim(block, block.shape[dim] - width, None, axis=dim), axis, forward
        )
        high = lax.ppermute(lax.slice_in_dim(block, 0, width, axis=dim), axis, backward)
        block = jnp.concatenate([low, block, high], axis=dim)
    return block


def passed_along(value, axis, by):
    peers = lax.axis_size(axis)
    return lax.ppermute(value, axis, [(i, (i + by) % peers) for i in range(peers)])


def first_diff(field, axis):
    count = field.shape[axis] - 6

    def part(offset):
        return lax.slice_in_dim(field, 3 + offset, 3 + offset + count, axis=axis)

    return (45.0 * (part(1) - part(-1)) - 9.0 * (part(2) - part(-2)) + (part(3) - part(-3))) / 60.0


def second_diff(field, axis):
    count = field.shape[axis] - 6

    def part(offset):
        return lax.slice_in_dim(field, 3 + offset, 3 + offset + count, axis=axis)

    return (
        -490.0 * part(0)
        + 270.0 * (part(1) + part(-1))
        - 27.0 * (part(2) + part(-2))
        + 2.0 * (part(3) + part(-3))
    ) / 180.0


def inner(field, axes):
    for axis in axes:
        field = lax.slice_in_dim(field, 3, field.shape[axis] - 3, axis=axis)
    return field


def tendency(padded, forcing, xfrac, inv_width):
    grads = [
        inner(first_diff(padded, 1), (2, 3)),
        inner(first_diff(padded, 2), (1, 3)),
        inner(first_diff(padded, 3), (1, 2)),
    ]
    vectors = padded[:6]
    curv = [
        inner(second_diff(vectors, 1), (2, 3)),
        inner(second_diff(vectors, 2), (1, 3)),
        inner(second_diff(vectors, 3), (1, 2)),
    ]
    cross_xy = inner(first_diff(first_diff(vectors, 2), 1), (3,))
    cross_xz = inner(first_diff(first_diff(vectors, 3), 1), (2,))
    cross_yz = inner(first_diff(first_diff(vectors, 3), 2), (1,))
    center = inner(padded, (1, 2, 3))
    velx, vely, velz = (center[0], center[1], center[2])
    potx, poty = (center[3], center[4])

    def grad(axis, comp):
        return grads[axis][comp]

    def lapl(comp):
        return curv[0][comp] + curv[1][comp] + curv[2][comp]

    def grad_div(first):
        return (
            curv[0][first] + cross_xy[first + 1] + cross_xz[first + 2],
            cross_xy[first] + curv[1][first + 1] + cross_yz[first + 2],
            cross_xz[first] + cross_yz[first + 1] + curv[2][first + 2],
        )

    fieldx = grad(1, 5) - grad(2, 4)
    fieldy = grad(2, 3) - grad(0, 5)
    fieldz = grad(0, 4) - grad(1, 3) + 0.5
    potdiv = grad_div(3)
    currx = potdiv[0] - lapl(3)
    curry = potdiv[1] - lapl(4)
    currz = potdiv[2] - lapl(5)
    veldiv = grad_div(0)
    inv_rho = jnp.exp(-center[6])
    flow = -1.5 * xfrac
    shear_rate = -1.5 * inv_width

    def advect(comp):
        return velx * grad(0, comp) + (vely + flow) * grad(1, comp) + velz * grad(2, comp)

    divu = grad(0, 0) + grad(1, 1) + grad(2, 2)
    lorentz = (
        curry * fieldz - currz * fieldy,
        currz * fieldx - currx * fieldz,
        currx * fieldy - curry * fieldx,
    )
    emf = (
        vely * fieldz - velz * fieldy,
        velz * fieldx - velx * fieldz,
        velx * fieldy - vely * fieldx,
    )
    curr = (currx, curry, currz)
    rates = []
    for comp in range(3):
        rate = -advect(comp) - grad(comp, 6) + lorentz[comp] * inv_rho
        total = jnp.zeros_like(velx)
        for col in range(3):
            strain = 0.5 * (grad(col, comp) + grad(comp, col))
            if col == comp:
                strain = strain - divu / 3.0
            total = total + 2.0 * strain * grad(col, 6)
        rate = rate + 0.05 * (lapl(comp) + veldiv[comp] / 3.0 + total) + forcing[comp]
        if comp == 0:
            rate = rate + 2.0 * 0.5 * vely
        if comp == 1:
            rate = rate - 2.0 * 0.5 * velx - shear_rate * velx
        rates.append(rate)
    for comp in range(3):
        rate = emf[comp] - flow * grad(1, 3 + comp) - 0.05 * curr[comp]
        if comp == 0:
            rate = rate - shear_rate * poty
        rates.append(rate)
    rates.append(-advect(6) - divu)
    return jnp.stack(rates)


def per_device(state, register, forcing, y_shift):
    cells_x = state.shape[1]
    cells_y = state.shape[2]
    slabs_x = lax.axis_size("gx")
    slabs_y = lax.axis_size("yz")
    total_x = cells_x * slabs_x
    total_y = cells_y * slabs_y
    where_x = lax.axis_index("gx")
    extended = padded_2(state, (("gx", 1),), 3)
    lower = extended[:, :3]
    upper = extended[:, cells_x + 3 :]
    at_low = where_x == 0
    at_high = where_x == slabs_x - 1
    boundary = jnp.where(at_high, upper, lower)
    offset = y_shift[0]
    amount = jnp.where(at_high, total_y - offset, offset) % total_y
    whole_steps = amount // cells_y
    remainder = amount % cells_y
    levels = slabs_y.bit_length() - 1
    bit_list = list(range(levels))
    current = boundary
    for bit in bit_list:
        moved = passed_along(current, "yz", slabs_y - (1 << bit))
        current = jnp.where(whole_steps >> bit & 1 == 1, moved, current)
    following = passed_along(current, "yz", slabs_y - 1)
    joined = jnp.concatenate([current, following], axis=2)
    sheared = lax.dynamic_slice_in_dim(joined, remainder, cells_y, 2)
    lower = jnp.where(at_low, sheared, lower)
    upper = jnp.where(at_high, sheared, upper)
    extended = jnp.concatenate([lower, extended[:, 3 : cells_x + 3], upper], axis=1)
    padded = padded_2(extended, (("yz", 2),), 3)
    padded = jnp.concatenate([padded[:, :, :, -3:], padded, padded[:, :, :, :3]], axis=3)
    inv_width = 1.0 / total_x
    index = (where_x * cells_x + jnp.arange(cells_x)).astype(jnp.float32)
    xfrac = ((index + 0.5) * inv_width - 0.5).reshape(cells_x, 1, 1)
    rate = tendency(padded, forcing, xfrac, inv_width)
    new_register = -5.0 / 9.0 * register + 0.15 * rate
    new_state = state + 15.0 / 16.0 * new_register
    return (new_state, new_register)


def solution(mesh):
    return jax.shard_map(
        per_device,
        mesh=mesh,
        in_specs=(
            P(None, "gx", "yz", None),
            P(None, "gx", "yz", None),
            P(None, "gx", "yz", None),
            P(),
        ),
        out_specs=(P(None, "gx", "yz", None), P(None, "gx", "yz", None)),
        check_vma=False,
    )
```

profile of v0, /device:TPU:128, one launch (start us, length us, event | category | flops | bytes accessed | tf_op | source)
XLA Modules:
  0.0 145.2 jit_solution(16482127989744994495)
XLA Ops:
  0.6 1.1 copy.51
  1.8 9.1 %collective-permute-start.1 = (f32[7,3,8,128]{3,1,2,0:T(4,128)S(1)}, f32[7,3,8,128]{3,1,2,0:T(4,128)S(1)}, u32[]{:S(2)}, u32[]{:S(2)}) collective-permute-start(f32[7,3,8,128]{3,1,2,0:T(4,128)S(1)} %get-tuple-element.29), channel_id=1, source_target_pairs={{0,1},{1,2},{2,3},{3,0},{4,5},{5,6},{6,7},{7,4},{8,9},{9,10},{10,1... | collective-permute-start | bytes 258056 | tf_op jit(solution)/shard_map/ppermute | solution.py:13
  10.9 1.9 %collective-permute-start = (f32[7,3,8,128]{3,1,2,0:T(4,128)S(1)}, f32[7,3,8,128]{3,1,2,0:T(4,128)S(1)}, u32[]{:S(2)}, u32[]{:S(2)}) collective-permute-start(f32[7,3,8,128]{3,1,2,0:T(4,128)S(1)} %get-tuple-element.30), channel_id=1, source_target_pairs={{1,0},{2,1},{3,2},{0,3},{5,4},{6,5},{7,6},{4,7},{9,8},{10,9},{11,1... | collective-permute-start | bytes 258056 | tf_op jit(solution)/shard_map/ppermute | solution.py:16
  12.8 7.6 %collective-permute-done.1 = f32[7,3,8,128]{3,1,2,0:T(4,128)S(1)} collective-permute-done((f32[7,3,8,128]{3,1,2,0:T(4,128)S(1)}, f32[7,3,8,128]{3,1,2,0:T(4,128)S(1)}, u32[]{:S(2)}, u32[]{:S(2)}) %collective-permute-start.1) | collective-permute-done | bytes 86048 | tf_op jit(solution)/shard_map/ppermute | solution.py:13
  20.4 8.2 %collective-permute-done = f32[7,3,8,128]{3,1,2,0:T(4,128)S(1)} collective-permute-done((f32[7,3,8,128]{3,1,2,0:T(4,128)S(1)}, f32[7,3,8,128]{3,1,2,0:T(4,128)S(1)}, u32[]{:S(2)}, u32[]{:S(2)}) %collective-permute-start) | collective-permute-done | bytes 86048 | tf_op jit(solution)/shard_map/ppermute | solution.py:16
  28.7 2.1 %collective-permute-start.2 = (f32[7,3,8,128]{3,1,2,0:T(4,128)S(1)}, f32[7,3,8,128]{3,1,2,0:T(4,128)S(1)}, u32[]{:S(2)}, u32[]{:S(2)}) collective-permute-start(f32[7,3,8,128]{3,1,2,0:T(4,128)S(1)} %broadcast_select_fusion.1), channel_id=1, source_target_pairs={{0,508},{4,0},{8,4},{12,8},{16,12},{20,16},{24,20},{28,24},{32,28}... | collective-permute-start | bytes 258056 | tf_op jit(solution)/shard_map/ppermute | solution.py:23
  31.5 1.7 %collective-permute-done.2 = f32[7,3,8,128]{3,1,2,0:T(4,128)S(1)} collective-permute-done((f32[7,3,8,128]{3,1,2,0:T(4,128)S(1)}, f32[7,3,8,128]{3,1,2,0:T(4,128)S(1)}, u32[]{:S(2)}, u32[]{:S(2)}) %collective-permute-start.2) | collective-permute-done | bytes 86048 | tf_op jit(solution)/shard_map/ppermute | solution.py:23
  33.2 5.5 %collective-permute-start.3 = (f32[7,3,8,128]{3,1,2,0:T(4,128)S(1)}, f32[7,3,8,128]{3,1,2,0:T(4,128)S(1)}, u32[]{:S(2)}, u32[]{:S(2)}) collective-permute-start(f32[7,3,8,128]{3,1,2,0:T(4,128)S(1)} %broadcast_select_fusion.2), channel_id=1, source_target_pairs={{0,504},{4,508},{8,0},{12,4},{16,8},{20,12},{24,16},{28,20},{32,24... | collective-permute-start | bytes 258056 | tf_op jit(solution)/shard_map/ppermute | solution.py:23
  38.8 2.3 %collective-permute-done.3 = f32[7,3,8,128]{3,1,2,0:T(4,128)S(1)} collective-permute-done((f32[7,3,8,128]{3,1,2,0:T(4,128)S(1)}, f32[7,3,8,128]{3,1,2,0:T(4,128)S(1)}, u32[]{:S(2)}, u32[]{:S(2)}) %collective-permute-start.3) | collective-permute-done | bytes 86048 | tf_op jit(solution)/shard_map/ppermute | solution.py:23
  41.1 4.5 %collective-permute-start.4 = (f32[7,3,8,128]{3,1,2,0:T(4,128)S(1)}, f32[7,3,8,128]{3,1,2,0:T(4,128)S(1)}, u32[]{:S(2)}, u32[]{:S(2)}) collective-permute-start(f32[7,3,8,128]{3,1,2,0:T(4,128)S(1)} %broadcast_select_fusion.3), channel_id=1, source_target_pairs={{0,496},{4,500},{8,504},{12,508},{16,0},{20,4},{24,8},{28,12},{32,... | collective-permute-start | bytes 258056 | tf_op jit(solution)/shard_map/ppermute | solution.py:23
  45.7 3.7 %collective-permute-done.4 = f32[7,3,8,128]{3,1,2,0:T(4,128)S(1)} collective-permute-done((f32[7,3,8,128]{3,1,2,0:T(4,128)S(1)}, f32[7,3,8,128]{3,1,2,0:T(4,128)S(1)}, u32[]{:S(2)}, u32[]{:S(2)}) %collective-permute-start.4) | collective-permute-done | bytes 86048 | tf_op jit(solution)/shard_map/ppermute | solution.py:23
  49.4 4.9 %collective-permute-start.5 = (f32[7,3,8,128]{3,1,2,0:T(4,128)S(1)}, f32[7,3,8,128]{3,1,2,0:T(4,128)S(1)}, u32[]{:S(2)}, u32[]{:S(2)}) collective-permute-start(f32[7,3,8,128]{3,1,2,0:T(4,128)S(1)} %broadcast_select_fusion.4), channel_id=1, source_target_pairs={{0,480},{4,484},{8,488},{12,492},{16,496},{20,500},{24,504},{28,50... | collective-permute-start | bytes 258056 | tf_op jit(solution)/shard_map/ppermute | solution.py:23
  54.3 4.0 %collective-permute-done.5 = f32[7,3,8,128]{3,1,2,0:T(4,128)S(1)} collective-permute-done((f32[7,3,8,128]{3,1,2,0:T(4,128)S(1)}, f32[7,3,8,128]{3,1,2,0:T(4,128)S(1)}, u32[]{:S(2)}, u32[]{:S(2)}) %collective-permute-start.5) | collective-permute-done | bytes 86048 | tf_op jit(solution)/shard_map/ppermute | solution.py:23
  58.3 2.8 %collective-permute-start.6 = (f32[7,3,8,128]{3,1,2,0:T(4,128)S(1)}, f32[7,3,8,128]{3,1,2,0:T(4,128)S(1)}, u32[]{:S(2)}, u32[]{:S(2)}) collective-permute-start(f32[7,3,8,128]{3,1,2,0:T(4,128)S(1)} %broadcast_select_fusion.5), channel_id=1, source_target_pairs={{0,448},{4,452},{8,456},{12,460},{16,464},{20,468},{24,472},{28,47... | collective-permute-start | bytes 258056 | tf_op jit(solution)/shard_map/ppermute | solution.py:23
  61.1 5.8 %collective-permute-done.6 = f32[7,3,8,128]{3,1,2,0:T(4,128)S(1)} collective-permute-done((f32[7,3,8,128]{3,1,2,0:T(4,128)S(1)}, f32[7,3,8,128]{3,1,2,0:T(4,128)S(1)}, u32[]{:S(2)}, u32[]{:S(2)}) %collective-permute-start.6) | collective-permute-done | bytes 86048 | tf_op jit(solution)/shard_map/ppermute | solution.py:23
  66.9 3.1 %collective-permute-start.7 = (f32[7,3,8,128]{3,1,2,0:T(4,128)S(1)}, f32[7,3,8,128]{3,1,2,0:T(4,128)S(1)}, u32[]{:S(2)}, u32[]{:S(2)}) collective-permute-start(f32[7,3,8,128]{3,1,2,0:T(4,128)S(1)} %broadcast_select_fusion.6), channel_id=1, source_target_pairs={{0,384},{4,388},{8,392},{12,396},{16,400},{20,404},{24,408},{28,41... | collective-permute-start | bytes 258056 | tf_op jit(solution)/shard_map/ppermute | solution.py:23
  70.1 5.3 %collective-permute-done.7 = f32[7,3,8,128]{3,1,2,0:T(4,128)S(1)} collective-permute-done((f32[7,3,8,128]{3,1,2,0:T(4,128)S(1)}, f32[7,3,8,128]{3,1,2,0:T(4,128)S(1)}, u32[]{:S(2)}, u32[]{:S(2)}) %collective-permute-start.7) | collective-permute-done | bytes 86048 | tf_op jit(solution)/shard_map/ppermute | solution.py:23
  75.4 2.6 %collective-permute-start.8 = (f32[7,3,8,128]{3,1,2,0:T(4,128)S(1)}, f32[7,3,8,128]{3,1,2,0:T(4,128)S(1)}, u32[]{:S(2)}, u32[]{:S(2)}) collective-permute-start(f32[7,3,8,128]{3,1,2,0:T(4,128)S(1)} %broadcast_select_fusion.7), channel_id=1, source_target_pairs={{0,256},{4,260},{8,264},{12,268},{16,272},{20,276},{24,280},{28,28... | collective-permute-start | bytes 258056 | tf_op jit(solution)/shard_map/ppermute | solution.py:23
  78.1 7.2 %collective-permute-done.8 = f32[7,3,8,128]{3,1,2,0:T(4,128)S(1)} collective-permute-done((f32[7,3,8,128]{3,1,2,0:T(4,128)S(1)}, f32[7,3,8,128]{3,1,2,0:T(4,128)S(1)}, u32[]{:S(2)}, u32[]{:S(2)}) %collective-permute-start.8) | collective-permute-done | bytes 86048 | tf_op jit(solution)/shard_map/ppermute | solution.py:23
  85.3 17.7 %collective-permute-start.9 = (f32[7,3,8,128]{3,1,2,0:T(4,128)S(1)}, f32[7,3,8,128]{3,1,2,0:T(4,128)S(1)}, u32[]{:S(2)}, u32[]{:S(2)}) collective-permute-start(f32[7,3,8,128]{3,1,2,0:T(4,128)S(1)} %broadcast_select_fusion.8), channel_id=1, source_target_pairs={{0,508},{4,0},{8,4},{12,8},{16,12},{20,16},{24,20},{28,24},{32,28}... | collective-permute-start | bytes 258056 | tf_op jit(solution)/shard_map/ppermute | solution.py:23
  103.0 2.3 %collective-permute-done.9 = f32[7,3,8,128]{3,1,2,0:T(4,128)S(1)} collective-permute-done((f32[7,3,8,128]{3,1,2,0:T(4,128)S(1)}, f32[7,3,8,128]{3,1,2,0:T(4,128)S(1)}, u32[]{:S(2)}, u32[]{:S(2)}) %collective-permute-start.9) | collective-permute-done | bytes 86048 | tf_op jit(solution)/shard_map/ppermute | solution.py:23
  105.5 9.8 %collective-permute-start.11 = (f32[7,22,3,128]{3,1,2,0:T(8,128)S(1)}, f32[7,22,3,128]{3,1,2,0:T(8,128)S(1)}, u32[]{:S(2)}, u32[]{:S(2)}) collective-permute-start(f32[7,22,3,128]{3,1,2,0:T(8,128)S(1)} %get-tuple-element.28), channel_id=1, source_target_pairs={{4,0},{8,4},{12,8},{16,12},{20,16},{24,20},{28,24},{32,28},{36,32}... | collective-permute-start | bytes 709640 | tf_op jit(solution)/shard_map/ppermute | solution.py:16
  115.3 1.9 %collective-permute-start.10 = (f32[7,22,3,128]{3,1,2,0:T(8,128)S(1)}, f32[7,22,3,128]{3,1,2,0:T(8,128)S(1)}, u32[]{:S(2)}, u32[]{:S(2)}) collective-permute-start(f32[7,22,3,128]{3,1,2,0:T(8,128)S(1)} %get-tuple-element.27), channel_id=1, source_target_pairs={{0,4},{4,8},{8,12},{12,16},{16,20},{20,24},{24,28},{28,32},{32,36}... | collective-permute-start | bytes 709640 | tf_op jit(solution)/shard_map/ppermute | solution.py:13
  117.3 1.8 %collective-permute-done.11 = f32[7,22,3,128]{3,1,2,0:T(8,128)S(1)} collective-permute-done((f32[7,22,3,128]{3,1,2,0:T(8,128)S(1)}, f32[7,22,3,128]{3,1,2,0:T(8,128)S(1)}, u32[]{:S(2)}, u32[]{:S(2)}) %collective-permute-start.11) | collective-permute-done | bytes 236576 | tf_op jit(solution)/shard_map/ppermute | solution.py:16
  119.1 9.8 %collective-permute-done.10 = f32[7,22,3,128]{3,1,2,0:T(8,128)S(1)} collective-permute-done((f32[7,22,3,128]{3,1,2,0:T(8,128)S(1)}, f32[7,22,3,128]{3,1,2,0:T(8,128)S(1)}, u32[]{:S(2)}, u32[]{:S(2)}) %collective-permute-start.10) | collective-permute-done | bytes 236576 | tf_op jit(solution)/shard_map/ppermute | solution.py:13
  129.5 1.3 pad_maximum_fusion
  131.5 1.0 fusion.7
  132.5 3.1 %pad_maximum_fusion.1 = (f32[7,22,14,131]{3,1,2,0:T(8,128)S(1)}, f32[7,22,14,131]{3,1,2,0:T(8,128)S(1)}) fusion(f32[7,22,14,3]{3,1,2,0:T(8,128)S(1)} %get-tuple-element.25, f32[7,22,3,128]{3,1,2,0:T(8,128)S(1)} %collective-permute-done.11, f32[7,3,8,128]{3,1,2,0:T(4,128)S(1)} %get-tuple-element.32, f32[7,16,8,128]{3,1,2,0:T(8,128)S(1)} %copy.51, ...), kind=kLoop, calls=%fused_computation.1 | loop fusion | flops 2824360 | bytes 3415104 | tf_op jit(solution)/shard_map/concatenate | solution.py:169
  135.6 1.4 fusion.29
  137.0 1.6 %fusion.18 = f32[7,22,14,128]{3,1,2,0:T(8,128)S(1)} fusion(f32[7,22,14,131]{3,1,2,0:T(8,128)S(1)} %get-tuple-element.24, f32[7,22,14,131]{3,1,2,0:T(8,128)S(1)} %get-tuple-element.23), kind=kLoop, calls=%fused_computation.32 | loop fusion | flops 2207744 | bytes 7727104 | tf_op jit(solution)/shard_map/div | solution.py:32
  139.0 0.9 fusion.1
  143.3 0.9 copy.52
  (35 shorter events, 6.4 us)
Async XLA Ops:
  1.8 18.6 %collective-permute-start.1 = (f32[7,3,8,128]{3,1,2,0:T(4,128)S(1)}, f32[7,3,8,128]{3,1,2,0:T(4,128)S(1)}, u32[]{:S(2)}, u32[]{:S(2)}) collective-permute-start(f32[7,3,8,128]{3,1,2,0:T(4,128)S(1)} %get-tuple-element.29), channel_id=1, source_target_pairs={{0,1},{1,2},{2,3},{3,0},{4,5},{5,6},{6,7},{7,4},{8,9},{9,10},{10,1... | collective-permute-start | bytes 258056 | tf_op jit(solution)/shard_map/ppermute | solution.py:13
  10.9 17.8 %collective-permute-start = (f32[7,3,8,128]{3,1,2,0:T(4,128)S(1)}, f32[7,3,8,128]{3,1,2,0:T(4,128)S(1)}, u32[]{:S(2)}, u32[]{:S(2)}) collective-permute-start(f32[7,3,8,128]{3,1,2,0:T(4,128)S(1)} %get-tuple-element.30), channel_id=1, source_target_pairs={{1,0},{2,1},{3,2},{0,3},{5,4},{6,5},{7,6},{4,7},{9,8},{10,9},{11,1... | collective-permute-start | bytes 258056 | tf_op jit(solution)/shard_map/ppermute | solution.py:16
  28.7 4.4 %collective-permute-start.2 = (f32[7,3,8,128]{3,1,2,0:T(4,128)S(1)}, f32[7,3,8,128]{3,1,2,0:T(4,128)S(1)}, u32[]{:S(2)}, u32[]{:S(2)}) collective-permute-start(f32[7,3,8,128]{3,1,2,0:T(4,128)S(1)} %broadcast_select_fusion.1), channel_id=1, source_target_pairs={{0,508},{4,0},{8,4},{12,8},{16,12},{20,16},{24,20},{28,24},{32,28}... | collective-permute-start | bytes 258056 | tf_op jit(solution)/shard_map/ppermute | solution.py:23
  33.2 7.9 %collective-permute-start.3 = (f32[7,3,8,128]{3,1,2,0:T(4,128)S(1)}, f32[7,3,8,128]{3,1,2,0:T(4,128)S(1)}, u32[]{:S(2)}, u32[]{:S(2)}) collective-permute-start(f32[7,3,8,128]{3,1,2,0:T(4,128)S(1)} %broadcast_select_fusion.2), channel_id=1, source_target_pairs={{0,504},{4,508},{8,0},{12,4},{16,8},{20,12},{24,16},{28,20},{32,24... | collective-permute-start | bytes 258056 | tf_op jit(solution)/shard_map/ppermute | solution.py:23
  41.1 8.2 %collective-permute-start.4 = (f32[7,3,8,128]{3,1,2,0:T(4,128)S(1)}, f32[7,3,8,128]{3,1,2,0:T(4,128)S(1)}, u32[]{:S(2)}, u32[]{:S(2)}) collective-permute-start(f32[7,3,8,128]{3,1,2,0:T(4,128)S(1)} %broadcast_select_fusion.3), channel_id=1, source_target_pairs={{0,496},{4,500},{8,504},{12,508},{16,0},{20,4},{24,8},{28,12},{32,... | collective-permute-start | bytes 258056 | tf_op jit(solution)/shard_map/ppermute | solution.py:23
  49.4 8.9 %collective-permute-start.5 = (f32[7,3,8,128]{3,1,2,0:T(4,128)S(1)}, f32[7,3,8,128]{3,1,2,0:T(4,128)S(1)}, u32[]{:S(2)}, u32[]{:S(2)}) collective-permute-start(f32[7,3,8,128]{3,1,2,0:T(4,128)S(1)} %broadcast_select_fusion.4), channel_id=1, source_target_pairs={{0,480},{4,484},{8,488},{12,492},{16,496},{20,500},{24,504},{28,50... | collective-permute-start | bytes 258056 | tf_op jit(solution)/shard_map/ppermute | solution.py:23
  58.3 8.6 %collective-permute-start.6 = (f32[7,3,8,128]{3,1,2,0:T(4,128)S(1)}, f32[7,3,8,128]{3,1,2,0:T(4,128)S(1)}, u32[]{:S(2)}, u32[]{:S(2)}) collective-permute-start(f32[7,3,8,128]{3,1,2,0:T(4,128)S(1)} %broadcast_select_fusion.5), channel_id=1, source_target_pairs={{0,448},{4,452},{8,456},{12,460},{16,464},{20,468},{24,472},{28,47... | collective-permute-start | bytes 258056 | tf_op jit(solution)/shard_map/ppermute | solution.py:23
  66.9 50.3 %copy-start.2 = (f32[3,16,8,128]{3,2,1,0:T(8,128)S(1)}, f32[3,16,8,128]{3,2,1,0:T(8,128)}, u32[]{:S(2)}) copy-start(f32[3,16,8,128]{3,2,1,0:T(8,128)} %param.6) | copy-start | bytes 589828
  66.9 8.4 %collective-permute-start.7 = (f32[7,3,8,128]{3,1,2,0:T(4,128)S(1)}, f32[7,3,8,128]{3,1,2,0:T(4,128)S(1)}, u32[]{:S(2)}, u32[]{:S(2)}) collective-permute-start(f32[7,3,8,128]{3,1,2,0:T(4,128)S(1)} %broadcast_select_fusion.6), channel_id=1, source_target_pairs={{0,384},{4,388},{8,392},{12,396},{16,400},{20,404},{24,408},{28,41... | collective-permute-start | bytes 258056 | tf_op jit(solution)/shard_map/ppermute | solution.py:23
  75.4 9.8 %collective-permute-start.8 = (f32[7,3,8,128]{3,1,2,0:T(4,128)S(1)}, f32[7,3,8,128]{3,1,2,0:T(4,128)S(1)}, u32[]{:S(2)}, u32[]{:S(2)}) collective-permute-start(f32[7,3,8,128]{3,1,2,0:T(4,128)S(1)} %broadcast_select_fusion.7), channel_id=1, source_target_pairs={{0,256},{4,260},{8,264},{12,268},{16,272},{20,276},{24,280},{28,28... | collective-permute-start | bytes 258056 | tf_op jit(solution)/shard_map/ppermute | solution.py:23
  85.3 20.0 %collective-permute-start.9 = (f32[7,3,8,128]{3,1,2,0:T(4,128)S(1)}, f32[7,3,8,128]{3,1,2,0:T(4,128)S(1)}, u32[]{:S(2)}, u32[]{:S(2)}) collective-permute-start(f32[7,3,8,128]{3,1,2,0:T(4,128)S(1)} %broadcast_select_fusion.8), channel_id=1, source_target_pairs={{0,508},{4,0},{8,4},{12,8},{16,12},{20,16},{24,20},{28,24},{32,28}... | collective-permute-start | bytes 258056 | tf_op jit(solution)/shard_map/ppermute | solution.py:23
  105.5 13.6 %collective-permute-start.11 = (f32[7,22,3,128]{3,1,2,0:T(8,128)S(1)}, f32[7,22,3,128]{3,1,2,0:T(8,128)S(1)}, u32[]{:S(2)}, u32[]{:S(2)}) collective-permute-start(f32[7,22,3,128]{3,1,2,0:T(8,128)S(1)} %get-tuple-element.28), channel_id=1, source_target_pairs={{4,0},{8,4},{12,8},{16,12},{20,16},{24,20},{28,24},{32,28},{36,32}... | collective-permute-start | bytes 709640 | tf_op jit(solution)/shard_map/ppermute | solution.py:16
  115.3 13.7 %collective-permute-start.10 = (f32[7,22,3,128]{3,1,2,0:T(8,128)S(1)}, f32[7,22,3,128]{3,1,2,0:T(8,128)S(1)}, u32[]{:S(2)}, u32[]{:S(2)}) collective-permute-start(f32[7,22,3,128]{3,1,2,0:T(8,128)S(1)} %get-tuple-element.27), channel_id=1, source_target_pairs={{0,4},{4,8},{8,12},{12,16},{16,20},{20,24},{24,28},{28,32},{32,36}... | collective-permute-start | bytes 709640 | tf_op jit(solution)/shard_map/ppermute | solution.py:13
  141.9 1.0 copy-start
  142.0 1.1 copy-start.1
where the time goes:
time: 146 us; the launch traced here: 145 us
  starting transfers between devices  66 us (45%)
  waiting for transfers between devices  59.8 us (41%)
  other arithmetic  13.6 us (9%)
  local copies, waits for them, and re-layouts  4.11 us (3%)
  between operations  1.69 us (1%)
    ppermute x8, starting transfers between devices, passed_along(): lax.ppermute(value, axis, [(i, (i + by) % peers) for i in range(peers)])  43.3 us
    ppermute x8, waiting for transfers between devices, passed_along(): lax.ppermute(value, axis, [(i, (i + by) % peers) for i in range(peers)])  32.2 us
    ppermute x2, waiting for transfers between devices, padded_2(): lax.ppermute(lax.slice_in_dim(block, block.shape[dim] - width, None, axis...  17.4 us
    ppermute x2, starting transfers between devices, padded_2(): lax.ppermute(lax.slice_in_dim(block, 0, width, axis=dim), axis, backward)  11.7 us
    ppermute x2, starting transfers between devices, padded_2(): lax.ppermute(lax.slice_in_dim(block, block.shape[dim] - width, None, axis...  11 us
    ppermute x2, waiting for transfers between devices, padded_2(): lax.ppermute(lax.slice_in_dim(block, 0, width, axis=dim), axis, backward)  10.1 us
    concatenate x2, other arithmetic, per_device(): jnp.concatenate([padded[:, :, :, -3:], padded, padded[:, :, :, :3]], axis=3)  4.31 us
    div x6, other arithmetic, first_diff(): (45.0 * (part(1) - part(-1)) - 9.0 * (part(2) - part(-2)) + (part(3) - pa...  3.94 us
  transfers between devices with their start and end apart: 12, of which 12 were waited for; matrix products, arithmetic and copies ran while one was open for 0% of the time, Pallas kernels for 0%

commit v1 on v0

v1 whole, which is shorter than its diff:
```python
import functools

import jax
import jax.numpy as jnp
from jax import lax
from jax.experimental import pallas as pl
from jax.experimental.pallas import tpu as pltpu
from jax.sharding import PartitionSpec as P

MESH = pl.DeviceIdType.MESH
ANY = pl.BlockSpec(memory_space=pl.ANY)
VMEM = pl.BlockSpec(memory_space=pltpu.VMEM)


def exchange(steps, slabs_x, slabs_y, state, out, send, recv, own):
    gx = lax.axis_index("gx")
    yz = lax.axis_index("yz")
    planes, rows = state.shape[1], state.shape[2]
    first = (gx == 0).astype(jnp.int32)
    last = (gx == slabs_x - 1).astype(jnp.int32)
    above = {"yz": lax.rem(yz + (slabs_y - steps) * last, slabs_y), "gx": lax.rem(gx + 1, slabs_x)}
    below = {"yz": lax.rem(yz + steps * first, slabs_y), "gx": lax.rem(gx + slabs_x - 1, slabs_x)}
    right = {"yz": lax.rem(yz + 1, slabs_y)}
    left = {"yz": lax.rem(yz + slabs_y - 1, slabs_y)}

    block = pltpu.make_async_copy(state, out.at[:, pl.ds(3, planes), pl.ds(rows, rows)], own)
    block.start()
    barrier = pltpu.get_barrier_semaphore()
    for peer in (above, below, right, left):
        pl.semaphore_signal(barrier, inc=1, device_id=peer, device_id_type=MESH)
    pl.semaphore_wait(barrier, 4)

    def copy(slot, source, target, peer):
        return pltpu.make_async_remote_copy(
            src_ref=source, dst_ref=target, send_sem=send.at[slot], recv_sem=recv.at[slot],
            device_id=peer, device_id_type=MESH)

    middle = pl.ds(rows, rows)
    low, high = pl.ds(0, 3), pl.ds(planes + 3, 3)
    ups = copy(0, state.at[:, pl.ds(planes - 3, 3)], out.at[:, low, middle], above)
    downs = copy(1, state.at[:, pl.ds(0, 3)], out.at[:, high, middle], below)
    ups.start()
    downs.start()
    inner = pl.ds(3, planes)
    rights = copy(2, state.at[:, :, pl.ds(rows - 3, 3)], out.at[:, inner, pl.ds(rows - 3, 3)], right)
    lefts = copy(3, state.at[:, :, pl.ds(0, 3)], out.at[:, inner, pl.ds(2 * rows, 3)], left)
    rights.start()
    lefts.start()
    later = []
    for k, (cross, at) in enumerate(((ups, low), (downs, high))):
        cross.wait_recv()
        for j, (target, peer) in enumerate(((0, right), (2 * rows, left))):
            c = copy(4 + 2 * k + j, out.at[:, at, middle], out.at[:, at, pl.ds(target, rows)], peer)
            c.start()
            later.append(c)
    ups.wait_send()
    downs.wait_send()
    rights.wait()
    lefts.wait()
    for c in later:
        c.wait()
    block.wait()


def extended(steps, slabs_x, slabs_y, state):
    fields, planes, rows, lanes = state.shape
    return pl.pallas_call(
        functools.partial(exchange, steps, slabs_x, slabs_y),
        out_shape=pltpu.VMEM((fields, planes + 6, 3 * rows, lanes), state.dtype),
        in_specs=[ANY],
        out_specs=VMEM,
        scratch_shapes=[
            pltpu.SemaphoreType.DMA((8,)),
            pltpu.SemaphoreType.DMA((8,)),
            pltpu.SemaphoreType.DMA,
        ],
        compiler_params=pltpu.CompilerParams(collective_id=steps, has_side_effects=True),
        name="extended",
    )(state)


def first_diff(low, high):
    return 0.75 * (high[0] - low[0]) - 0.15 * (high[1] - low[1]) + (1.0 / 60.0) * (high[2] - low[2])


def second_diff(center, *pairs):
    near, mid, far = (sum(high[k] + low[k] for low, high in pairs) for k in range(3))
    return (-490.0 / 180.0 * len(pairs)) * center + 1.5 * near - 0.15 * mid + (1.0 / 90.0) * far


def update(slabs_x, y_shift, ext, register, forcing, new_state, new_register, part):
    fields, planes, rows, lanes = new_state.shape
    gx = lax.axis_index("gx")
    offset = y_shift[0]
    left_over = lax.rem(offset + rows // 2, rows) - rows // 2

    def shear(at, by):
        for f in range(fields):
            for m in range(3):
                top = ext[f, at + m, pl.ds(rows - 3 + by, rows)]
                end = ext[f, at + m, pl.ds(rows + 3 + by, rows)]
                ext[f, at + m, pl.ds(rows - 3, rows)] = top
                ext[f, at + m, pl.ds(rows + 3, rows)] = end

    @pl.when(gx == 0)
    def _():
        shear(0, left_over)

    @pl.when(gx == slabs_x - 1)
    def _():
        shear(planes + 3, -left_over)

    def y_near(f, x):
        return tuple([ext[f, x, pl.ds(rows + sign * k, rows)] for k in (1, 2, 3)] for sign in (-1, 1))

    def x_near(f, x):
        return tuple([ext[f, x + sign * k, pl.ds(rows, rows)] for k in (1, 2, 3)] for sign in (-1, 1))

    def z_near(value):
        return (
            [pltpu.roll(value, k, 1) for k in (1, 2, 3)],
            [pltpu.roll(value, lanes - k, 1) for k in (1, 2, 3)],
        )

    def center(f, x):
        return ext[f, x, pl.ds(rows, rows)]

    def part_near(k, x):
        return tuple([part[k, x + sign * m] for m in (1, 2, 3)] for sign in (-1, 1))

    @pl.loop(0, planes + 6)
    def _(x):
        for k, f in ((0, 0), (3, 3)):
            dy = first_diff(*y_near(f + 1, x))
            dz = first_diff(*z_near(center(f + 2, x)))
            part[k, x] = first_diff(*y_near(f, x))
            part[k + 1, x] = dy
            part[k + 2, x] = dy + dz

    inv_width = 1.0 / (slabs_x * planes)
    shear_rate = -1.5 * inv_width

    @pl.loop(0, planes)
    def _(p):
        x = p + 3
        xfrac = ((gx * planes + p).astype(jnp.float32) + 0.5) * inv_width - 0.5
        flow = -1.5 * xfrac
        cen = [center(f, x) for f in range(fields)]
        nx = [x_near(f, x) for f in range(fields)]
        ny = [y_near(f, x) for f in range(fields)]
        nz = [z_near(cen[f]) for f in range(fields)]
        dx = [first_diff(*nx[f]) for f in range(fields)]
        dz = [first_diff(*nz[f]) for f in range(fields)]
        dy = [part[f, x] if f in (0, 1, 3, 4) else first_diff(*ny[f]) for f in range(fields)]
        sums = [first_diff(*part_near(k, x)) for k in (0, 2, 3, 5)]
        vel = cen[:3]
        carried = vel[1] + flow
        bx = dy[5] - dz[4]
        by = dz[3] - dx[5]
        bz = dx[4] - dy[3] + 0.5
        jx = sums[3] - second_diff(cen[3], ny[3], nz[3])
        jy = sums[2] + first_diff(*z_near(dy[5])) - second_diff(cen[4], nx[4], nz[4])
        jz = first_diff(*z_near(dx[3] + dy[4])) - second_diff(cen[5], nx[5], ny[5])
        curr = (jx, jy, jz)
        lorentz = (jy * bz - jz * by, jz * bx - jx * bz, jx * by - jy * bx)
        emf = (vel[1] * bz - vel[2] * by, vel[2] * bx - vel[0] * bz, vel[0] * by - vel[1] * bx)
        inv_rho = jnp.exp(-cen[6])
        divu = dx[0] + dy[1] + dz[2]
        rest = (
            sums[1],
            sums[0] + first_diff(*z_near(dy[2])),
            first_diff(*z_near(dx[0] + dy[1])),
        )
        grads = (dx, dy, dz)
        near = (nx, ny, nz)

        def advect(f):
            return vel[0] * dx[f] + carried * dy[f] + vel[2] * dz[f]

        rates = []
        for i in range(3):
            others = [near[a][i] for a in range(3) if a != i]
            viscous = second_diff(cen[i], *others) + (4.0 / 3.0) * second_diff(cen[i], near[i][i]) + rest[i] * (1.0 / 3.0)
            for j in range(3):
                if i == j:
                    strain = 2.0 * grads[i][i] - (2.0 / 3.0) * divu
                else:
                    strain = grads[j][i] + grads[i][j]
                viscous = viscous + strain * grads[j][6]
            rate = lorentz[i] * inv_rho - advect(i) - grads[i][6] + 0.05 * viscous + forcing[i, p]
            if i == 0:
                rate = rate + vel[1]
            if i == 1:
                rate = rate - (1.0 + shear_rate) * vel[0]
            rates.append(rate)
        for i in range(3):
            rate = emf[i] - flow * dy[3 + i] - 0.05 * curr[i]
            if i == 0:
                rate = rate - shear_rate * cen[4]
            rates.append(rate)
        rates.append(-advect(6) - divu)
        for f in range(fields):
            kept = (-5.0 / 9.0) * register[f, p] + 0.15 * rates[f]
            new_register[f, p] = kept
            new_state[f, p] = cen[f] + 0.9375 * kept


def per_device(state, register, forcing, y_shift):
    slabs_x = lax.axis_size("gx")
    slabs_y = lax.axis_size("yz")
    fields, planes, rows, lanes = state.shape
    whole = lax.div(y_shift[0] + rows // 2, rows)
    ext = lax.switch(
        lax.rem(whole, slabs_y),
        [functools.partial(extended, s, slabs_x, slabs_y) for s in range(slabs_y)],
        state,
    )
    ext = pltpu.with_memory_space_constraint(ext, pltpu.VMEM)
    return pl.pallas_call(
        functools.partial(update, slabs_x),
        out_shape=(jax.ShapeDtypeStruct(state.shape, state.dtype),) * 2,
        in_specs=[pl.BlockSpec(memory_space=pltpu.SMEM), VMEM, VMEM, VMEM],
        out_specs=(VMEM, VMEM),
        scratch_shapes=[pltpu.VMEM((6, planes + 6, rows, lanes), jnp.float32)],
        compiler_params=pltpu.CompilerParams(vmem_limit_bytes=40 * 2**20),
        name="update",
    )(y_shift, ext, register, forcing)


def solution(mesh):
    spec = P(None, "gx", "yz", None)
    return jax.shard_map(
        per_device,
        mesh=mesh,
        in_specs=(spec, spec, spec, P()),
        out_specs=(spec, spec),
        check_vma=False,
    )
```

time: 146 us -> 56.2 us (0.38)
  the two profiles are of different devices: /device:TPU:128 before, /device:TPU:96 now
where the time goes in v1:
time: 56.2 us; the launch traced here: 56.1 us
  Pallas kernels  54.4 us (97%)
  between operations  1.34 us (2%)
    pallas_call x1, Pallas kernels, extended(): pl.pallas_call(functools.partial(exchange, steps, slabs_x, slabs_y), out_...  49.2 us
    pallas_call x1, Pallas kernels, per_device(): pl.pallas_call(functools.partial(update, slabs_x), out_shape=(jax.ShapeDt...  5.15 us

profile of v1, /device:TPU:96, one launch (start us, length us, event | category | flops | bytes accessed | tf_op | source)
XLA Modules:
  0.0 56.1 jit_solution(56875425141731278)
XLA Ops:
  1.3 0.0 copy-start
  1.3 0.0 copy-start.1
  1.3 49.6 %conditional.1 = (f32[7,22,24,128]{3,2,1,0:T(8,128)S(1)}) conditional(s32[]{:T(128)} %clamp.3, f32[7,16,8,128]{3,2,1,0:T(8,128)} %param.132, f32[7,16,8,128]{3,2,1,0:T(8,128)} %param.132, f32[7,16,8,128]{3,2,1,0:T(8,128)} %param.132, f32[7,16,8,128]{3,2,1,0:T(8,128)} %param.132, ...), branch_computations={%region_0.0_spmd, %region_1.0_spmd, %region_2.0_spmd, %region_3.0_... | conditional | bytes 8 | solution.py:213
  1.4 49.2 %extended.171 = f32[7,22,24,128]{3,2,1,0:T(8,128)S(1)} custom-call(f32[7,16,8,128]{3,2,1,0:T(8,128)} %state.43), custom_call_target="tpu_custom_call" | custom-call | tf_op jit(solution)/shard_map/cond/branch_43_fun/extended/pallas_call | solution.py:67
  50.9 0.0 copy-done
  50.9 0.0 copy-done.1
  50.9 5.1 %update.1 = (f32[7,16,8,128]{3,2,1,0:T(8,128)}, f32[7,16,8,128]{3,2,1,0:T(8,128)}) custom-call(s32[1]{0:T(128)S(6)} %copy.134.y_shift, f32[7,22,24,128]{3,2,1,0:T(8,128)S(1)} %get-tuple-element.259.ext, f32[7,16,8,128]{3,2,1,0:T(8,128)S(1)} %copy-done, f32[3,16,8,128]{3,2,1,0:T(8,128)S(1)} %copy-done.1), custom_call_target="tpu_custom_call" | custom-call | tf_op jit(solution)/shard_map/update/pallas_call | solution.py:219
Async XLA Ops:
  1.3 49.6 %copy-start = (f32[7,16,8,128]{3,2,1,0:T(8,128)S(1)}, f32[7,16,8,128]{3,2,1,0:T(8,128)}, u32[]{:S(2)}) copy-start(f32[7,16,8,128]{3,2,1,0:T(8,128)} %register.1) | copy-start | bytes 1376260
  1.3 49.6 %copy-start.1 = (f32[3,16,8,128]{3,2,1,0:T(8,128)S(1)}, f32[3,16,8,128]{3,2,1,0:T(8,128)}, u32[]{:S(2)}) copy-start(f32[3,16,8,128]{3,2,1,0:T(8,128)} %forcing.1) | copy-start | bytes 589828

commit v2 on v1

--- a/solution.py
+++ b/solution.py
@@ -12,7 +12,13 @@
 VMEM = pl.BlockSpec(memory_space=pltpu.VMEM)
 
 
-def exchange(steps, slabs_x, slabs_y, state, out, send, recv, own):
+SPAN = 4
+BACK = 12
+SLOTS = 6
+PARTS = ((0, 3), (3, 2), (5, 2))
+
+
+def exchange(steps, slabs_x, slabs_y, state, out, ghost, send, recv, row_send, row_recv, far_send, far_recv, own, ready, near):
     gx = lax.axis_index("gx")
     yz = lax.axis_index("yz")
     planes, rows = state.shape[1], state.shape[2]
@@ -20,61 +26,153 @@
     last = (gx == slabs_x - 1).astype(jnp.int32)
     above = {"yz": lax.rem(yz + (slabs_y - steps) * last, slabs_y), "gx": lax.rem(gx + 1, slabs_x)}
     below = {"yz": lax.rem(yz + steps * first, slabs_y), "gx": lax.rem(gx + slabs_x - 1, slabs_x)}
-    right = {"yz": lax.rem(yz + 1, slabs_y)}
-    left = {"yz": lax.rem(yz + slabs_y - 1, slabs_y)}
+
+    def along(by):
+        return {"yz": lax.rem(yz + (slabs_y + by), slabs_y)}
+
+    def tell(semaphore, peer):
+        pl.semaphore_signal(semaphore, inc=1, device_id=peer, device_id_type=MESH)
+
+    def copy(source, target, send_sem, recv_sem, peer):
+        return pltpu.make_async_remote_copy(
+            src_ref=source, dst_ref=target, send_sem=send_sem, recv_sem=recv_sem,
+            device_id=peer, device_id_type=MESH)
 
     block = pltpu.make_async_copy(state, out.at[:, pl.ds(3, planes), pl.ds(rows, rows)], own)
+
+    def across(side, n):
+        start, count = PARTS[n]
+        source = state.at[pl.ds(start, count), pl.ds((planes - 3) * (1 - side), 3)]
+        target = ghost.at[side, pl.ds(start, count), :, pl.ds((2 + side) * rows, rows)]
+        return copy(source, target, far_send.at[side, n], far_recv.at[side, n], above if side == 0 else below)
+
+    ups = [across(0, n) for n in range(len(PARTS))]
+    downs = [across(1, n) for n in range(len(PARTS))]
+
+    def start(copies):
+        for c in copies:
+            c.start()
+
+    inner = pl.ds(3, planes)
+    sides = [
+        copy(state.at[:, :, pl.ds(rows - 3, 3)], out.at[:, inner, pl.ds(rows - 3, 3)], row_send.at[0], row_recv.at[0], along(1)),
+        copy(state.at[:, :, pl.ds(0, 3)], out.at[:, inner, pl.ds(2 * rows, 3)], row_send.at[1], row_recv.at[1], along(-1)),
+    ]
+
+    barrier = pltpu.get_barrier_semaphore()
+    far = slabs_x // 2
+    tell(barrier, along(1))
+    tell(barrier, along(-1))
+
+    @pl.when((gx == 0) | (gx == 1))
+    def _():
+        tell(barrier, above)
+
+    @pl.when((gx == 0) | (gx == slabs_x - 1))
+    def _():
+        tell(barrier, below)
+
+    @pl.when(gx == 0)
+    def _():
+        pl.semaphore_wait(barrier, 2)
+        start(sides)
+        pl.semaphore_wait(ready.at[0], 1)
+        start(ups)
+        pl.semaphore_wait(ready.at[1], 1)
+        start(downs)
+
+    @pl.when(gx == 1)
+    def _():
+        pl.semaphore_wait(barrier, 3)
+        start(downs)
+        tell(ready.at[0], below)
+        start(sides)
+        pl.semaphore_wait(ready.at[0], 1)
+        start(ups)
+
+    @pl.when(gx == slabs_x - 1)
+    def _():
+        pl.semaphore_wait(barrier, 3)
+        start(ups)
+        tell(ready.at[1], above)
+        start(sides)
+        pl.semaphore_wait(ready.at[1], 1)
+        start(downs)
+
+    @pl.when(gx == far)
+    def _():
+        pl.semaphore_wait(barrier, 4)
+        tell(ready.at[0], below)
+        tell(ready.at[1], above)
+        start(ups)
+        start(downs)
+        start(sides)
+
     block.start()
-    barrier = pltpu.get_barrier_semaphore()
-    for peer in (above, below, right, left):
-        pl.semaphore_signal(barrier, inc=1, device_id=peer, device_id_type=MESH)
-    pl.semaphore_wait(barrier, 4)
-
-    def copy(slot, source, target, peer):
-        return pltpu.make_async_remote_copy(
-            src_ref=source, dst_ref=target, send_sem=send.at[slot], recv_sem=recv.at[slot],
-            device_id=peer, device_id_type=MESH)
-
-    middle = pl.ds(rows, rows)
-    low, high = pl.ds(0, 3), pl.ds(planes + 3, 3)
-    ups = copy(0, state.at[:, pl.ds(planes - 3, 3)], out.at[:, low, middle], above)
-    downs = copy(1, state.at[:, pl.ds(0, 3)], out.at[:, high, middle], below)
-    ups.start()
-    downs.start()
-    inner = pl.ds(3, planes)
-    rights = copy(2, state.at[:, :, pl.ds(rows - 3, 3)], out.at[:, inner, pl.ds(rows - 3, 3)], right)
-    lefts = copy(3, state.at[:, :, pl.ds(0, 3)], out.at[:, inner, pl.ds(2 * rows, 3)], left)
-    rights.start()
-    lefts.start()
-    later = []
-    for k, (cross, at) in enumerate(((ups, low), (downs, high))):
-        cross.wait_recv()
-        for j, (target, peer) in enumerate(((0, right), (2 * rows, left))):
-            c = copy(4 + 2 * k + j, out.at[:, at, middle], out.at[:, at, pl.ds(target, rows)], peer)
-            c.start()
-            later.append(c)
-    ups.wait_send()
-    downs.wait_send()
-    rights.wait()
-    lefts.wait()
-    for c in later:
+    edge = (gx == 0) | (gx == slabs_x - 1)
+
+    @pl.when(edge)
+    def _():
+        for k in range(2):
+            tell(near.at[k], along(1))
+            tell(near.at[k], along(-1))
+            pl.semaphore_wait(near.at[k], 2)
+
+    def forward(side, n, k, by):
+        begin, count = PARTS[n]
+        fields = pl.ds(begin, count)
+        own_rows = pl.ds(pl.multiple_of((2 + side) * rows, rows), rows)
+        their_rows = pl.ds(pl.multiple_of((2 + side - by) * rows, rows), rows)
+        return copy(
+            ghost.at[side, fields, :, own_rows], ghost.at[side, fields, :, their_rows],
+            send.at[side, n, k], recv.at[side, n, k], along(by))
+
+    sooner = edge.astype(jnp.int32)
+    passes = ((sooner, gx == slabs_x - 1), (1 - sooner, gx == 0))
+    for side, sheared in passes:
+        for n, (begin, count) in enumerate(PARTS):
+            here = ghost.at[side, pl.ds(begin, count), :, pl.ds(pl.multiple_of((2 + side) * rows, rows), rows)]
+            copy(here, here, far_send.at[side, n], far_recv.at[side, n], along(1)).wait_recv()
+            for k, by in enumerate((1, -1)):
+                forward(side, n, k, by).start()
+
+            @pl.when(sheared)
+            def _():
+                for k, by in ((2, 2), (3, -2), (4, 6 * side - 3)):
+                    forward(side, n, k, by).start()
+    for c in ups + downs:
+        c.wait_send()
+    for c in sides:
         c.wait()
+    for side, sheared in passes:
+        for n in range(len(PARTS)):
+            for k, by in enumerate((1, -1)):
+                forward(side, n, k, by).wait()
+
+            @pl.when(sheared)
+            def _():
+                for k, by in ((2, 2), (3, -2), (4, 6 * side - 3)):
+                    forward(side, n, k, by).wait()
     block.wait()
 
 
 def extended(steps, slabs_x, slabs_y, state):
     fields, planes, rows, lanes = state.shape
+    parts = len(PARTS)
+    dma = pltpu.SemaphoreType.DMA
     return pl.pallas_call(
         functools.partial(exchange, steps, slabs_x, slabs_y),
-        out_shape=pltpu.VMEM((fields, planes + 6, 3 * rows, lanes), state.dtype),
+        out_shape=(
+            pltpu.VMEM((fields, planes + 6, 3 * rows, lanes), state.dtype),
+            pltpu.VMEM((2, fields, 3, SLOTS * rows, lanes), state.dtype),
+        ),
         in_specs=[ANY],
-        out_specs=VMEM,
+        out_specs=(VMEM, VMEM),
         scratch_shapes=[
-            pltpu.SemaphoreType.DMA((8,)),
-            pltpu.SemaphoreType.DMA((8,)),
-            pltpu.SemaphoreType.DMA,
+            dma((2, parts, 5)), dma((2, parts, 5)), dma((2,)), dma((2,)), dma((2, parts)), dma((2, parts)), dma,
+            pltpu.SemaphoreType.REGULAR((2,)), pltpu.SemaphoreType.REGULAR((2,)),
         ],
-        compiler_params=pltpu.CompilerParams(collective_id=steps, has_side_effects=True),
+        compiler_params=pltpu.CompilerParams(collective_id=steps // SPAN, has_side_effects=True),
         name="extended",
     )(state)
 
@@ -88,27 +186,18 @@
     return (-490.0 / 180.0 * len(pairs)) * center + 1.5 * near - 0.15 * mid + (1.0 / 90.0) * far
 
 
-def update(slabs_x, y_shift, ext, register, forcing, new_state, new_register, part):
+def update(slabs_x, y_shift, ghost, ext_in, register, forcing, new_state, new_register, ext, part):
     fields, planes, rows, lanes = new_state.shape
     gx = lax.axis_index("gx")
-    offset = y_shift[0]
-    left_over = lax.rem(offset + rows // 2, rows) - rows // 2
-
-    def shear(at, by):
+    left_over = lax.rem(y_shift[0] + BACK, SPAN * rows) - BACK
+    by = (jnp.where(gx == 0, left_over, 0), jnp.where(gx == slabs_x - 1, -left_over, 0))
+    for side in range(2):
+        start = (2 + side) * rows + by[side]
         for f in range(fields):
             for m in range(3):
-                top = ext[f, at + m, pl.ds(rows - 3 + by, rows)]
-                end = ext[f, at + m, pl.ds(rows + 3 + by, rows)]
-                ext[f, at + m, pl.ds(rows - 3, rows)] = top
-                ext[f, at + m, pl.ds(rows + 3, rows)] = end
-
-    @pl.when(gx == 0)
-    def _():
-        shear(0, left_over)
-
-    @pl.when(gx == slabs_x - 1)
-    def _():
-        shear(planes + 3, -left_over)
+                at = side * (planes + 3) + m
+                ext[f, at, pl.ds(rows - 3, rows)] = ghost[side, f, m, pl.ds(start - 3, rows)]
+                ext[f, at, pl.ds(rows + 3, rows)] = ghost[side, f, m, pl.ds(start + 3, rows)]
 
     def y_near(f, x):
         return tuple([ext[f, x, pl.ds(rows + sign * k, rows)] for k in (1, 2, 3)] for sign in (-1, 1))
@@ -209,22 +298,24 @@
     slabs_x = lax.axis_size("gx")
     slabs_y = lax.axis_size("yz")
     fields, planes, rows, lanes = state.shape
-    whole = lax.div(y_shift[0] + rows // 2, rows)
-    ext = lax.switch(
-        lax.rem(whole, slabs_y),
-        [functools.partial(extended, s, slabs_x, slabs_y) for s in range(slabs_y)],
+    ext, ghost = lax.switch(
+        lax.rem(lax.div(y_shift[0] + BACK, SPAN * rows), slabs_y // SPAN),
+        [functools.partial(extended, s, slabs_x, slabs_y) for s in range(0, slabs_y, SPAN)],
         state,
     )
     ext = pltpu.with_memory_space_constraint(ext, pltpu.VMEM)
-    return pl.pallas_call(
+    ghost = pltpu.with_memory_space_constraint(ghost, pltpu.VMEM)
+    new_state, new_register, _ = pl.pallas_call(
         functools.partial(update, slabs_x),
-        out_shape=(jax.ShapeDtypeStruct(state.shape, state.dtype),) * 2,
-        in_specs=[pl.BlockSpec(memory_space=pltpu.SMEM), VMEM, VMEM, VMEM],
-        out_specs=(VMEM, VMEM),
+        out_shape=(jax.ShapeDtypeStruct(state.shape, state.dtype),) * 2 + (pltpu.VMEM(ext.shape, ext.dtype),),
+        in_specs=[pl.BlockSpec(memory_space=pltpu.SMEM), VMEM, VMEM, VMEM, VMEM],
+        out_specs=(VMEM, VMEM, VMEM),
+        input_output_aliases={2: 2},
         scratch_shapes=[pltpu.VMEM((6, planes + 6, rows, lanes), jnp.float32)],
         compiler_params=pltpu.CompilerParams(vmem_limit_bytes=40 * 2**20),
         name="update",
-    )(y_shift, ext, register, forcing)
+    )(y_shift, ghost, ext, register, forcing)
+    return new_state, new_register
 
 
 def solution(mesh):

time: 56.2 us -> 40.8 us (0.73)
  the two profiles are of different devices: /device:TPU:96 before, /device:TPU:1 now
where the time goes in v2:
time: 40.8 us; the launch traced here: 40.7 us
  Pallas kernels  38.2 us (94%)
  between operations  1.33 us (3%)
  local copies, waits for them, and re-layouts  0.93 us (2%)
    pallas_call x1, Pallas kernels, extended(): pl.pallas_call(functools.partial(exchange, steps, slabs_x, slabs_y), out_...  33.1 us
    pallas_call x1, Pallas kernels, per_device(): pl.pallas_call(functools.partial(update, slabs_x), out_shape=(jax.ShapeDt...  5.1 us
    unnamed x4, local copies, waits for them, and re-layouts  0.93 us

profile of v2, /device:TPU:1, one launch (start us, length us, event | category | flops | bytes accessed | tf_op | source)
XLA Modules:
  0.0 40.7 jit_solution(3801747462620692339)
XLA Ops:
  1.3 0.0 copy-start
  1.3 33.3 %conditional.1 = ((f32[7,22,24,128]{3,2,1,0:T(8,128)S(1)}, f32[2,7,3,48,128]{4,3,2,1,0:T(8,128)S(1)})) conditional(s32[]{:T(128)} %clamp.3, f32[7,16,8,128]{3,2,1,0:T(8,128)} %param.36, f32[7,16,8,128]{3,2,1,0:T(8,128)} %param.36, f32[7,16,8,128]{3,2,1,0:T(8,128)} %param.36, f32[7,16,8,128]{3,2,1,0:T(8,128)} %param.36, ...), branch_computations={%region_0.0_spmd, %region_1.0_spmd, %region_2.0_spmd, %region_3.0_... | conditional | bytes 8 | solution.py:301
  1.4 33.1 %extended.46 = (f32[7,22,24,128]{3,2,1,0:T(8,128)S(1)}, f32[2,7,3,48,128]{4,3,2,1,0:T(8,128)S(1)}) custom-call(f32[7,16,8,128]{3,2,1,0:T(8,128)} %state.14), custom_call_target="tpu_custom_call" | custom-call | tf_op jit(solution)/shard_map/cond/branch_14_fun/extended/pallas_call | solution.py:163
  34.6 0.0 copy-done
  34.6 0.0 copy-start.1
  34.6 0.9 %copy-done.1 = f32[3,16,8,128]{3,2,1,0:T(8,128)S(1)} copy-done((f32[3,16,8,128]{3,2,1,0:T(8,128)S(1)}, f32[3,16,8,128]{3,2,1,0:T(8,128)}, u32[]{:S(2)}) %copy-start.1) | copy-done | bytes 196632
  35.6 5.1 %update.1 = (f32[7,16,8,128]{3,2,1,0:T(8,128)}, f32[7,16,8,128]{3,2,1,0:T(8,128)}, f32[7,22,24,128]{3,2,1,0:T(8,128)S(1)}) custom-call(s32[1]{0:T(128)S(6)} %copy.72.y_shift, f32[2,7,3,48,128]{4,3,2,1,0:T(8,128)S(1)} %get-tuple-element.38.ghost, f32[7,22,24,128]{3,2,1,0:T(8,128)S(1)} %get-tuple-element.39.ext_in, ...), custom_call_target="tpu_custom_call", output_to_operand_aliasing={{2}: (2, {})} | custom-call | tf_op jit(solution)/shard_map/update/pallas_call | solution.py:308
Async XLA Ops:
  1.3 33.3 %copy-start = (f32[7,16,8,128]{3,2,1,0:T(8,128)S(1)}, f32[7,16,8,128]{3,2,1,0:T(8,128)}, u32[]{:S(2)}) copy-start(f32[7,16,8,128]{3,2,1,0:T(8,128)} %register.1) | copy-start | bytes 1376260
  34.6 0.9 %copy-start.1 = (f32[3,16,8,128]{3,2,1,0:T(8,128)S(1)}, f32[3,16,8,128]{3,2,1,0:T(8,128)}, u32[]{:S(2)}) copy-start(f32[3,16,8,128]{3,2,1,0:T(8,128)} %forcing.1) | copy-start | bytes 589828

commit v3 on v2

--- a/solution.py
+++ b/solution.py
@@ -13,19 +13,25 @@
 
 
 SPAN = 4
-BACK = 12
-SLOTS = 6
-PARTS = ((0, 3), (3, 2), (5, 2))
-
-
-def exchange(steps, slabs_x, slabs_y, state, out, ghost, send, recv, row_send, row_recv, far_send, far_recv, own, ready, near):
+BACK = 16
+BASE = 3
+SLOTS = 2 * BASE + 1
+HALOED = 4
+
+
+def exchange(
+    steps, slabs_x, slabs_y, state, out, ghost, far_send, far_recv, row_send, row_recv, halo_send, halo_recv,
+    shear_send, shear_recv, pass_recv, own, ready, near
+):
     gx = lax.axis_index("gx")
     yz = lax.axis_index("yz")
-    planes, rows = state.shape[1], state.shape[2]
+    fields, planes, rows = state.shape[:3]
     first = (gx == 0).astype(jnp.int32)
     last = (gx == slabs_x - 1).astype(jnp.int32)
     above = {"yz": lax.rem(yz + (slabs_y - steps) * last, slabs_y), "gx": lax.rem(gx + 1, slabs_x)}
     below = {"yz": lax.rem(yz + steps * first, slabs_y), "gx": lax.rem(gx + slabs_x - 1, slabs_x)}
+    core = lax.rem(yz, 2)
+    twin = 1 - 2 * core
 
     def along(by):
         return {"yz": lax.rem(yz + (slabs_y + by), slabs_y)}
@@ -38,29 +44,35 @@
             src_ref=source, dst_ref=target, send_sem=send_sem, recv_sem=recv_sem,
             device_id=peer, device_id_type=MESH)
 
-    block = pltpu.make_async_copy(state, out.at[:, pl.ds(3, planes), pl.ds(rows, rows)], own)
-
-    def across(side, n):
-        start, count = PARTS[n]
-        source = state.at[pl.ds(start, count), pl.ds((planes - 3) * (1 - side), 3)]
-        target = ghost.at[side, pl.ds(start, count), :, pl.ds((2 + side) * rows, rows)]
-        return copy(source, target, far_send.at[side, n], far_recv.at[side, n], above if side == 0 else below)
-
-    ups = [across(0, n) for n in range(len(PARTS))]
-    downs = [across(1, n) for n in range(len(PARTS))]
-
-    def start(copies):
-        for c in copies:
-            c.start()
+    every = pl.ds(0, fields)
+
+    def one(field):
+        return 0 if field is every else field
+
+    def slot(side, field, at):
+        return ghost.at[side, field, :, pl.ds(pl.multiple_of(at * rows, rows), rows)]
+
+    def across(side, field):
+        source = state.at[field, pl.ds((planes - 3) * (1 - side), 3)]
+        return copy(source, slot(side, field, BASE), far_send.at[side], far_recv.at[side, one(field)], above if side == 0 else below)
+
+    def cross(*sides):
+        @pl.loop(0, fields)
+        def _(field):
+            for side in sides:
+                across(side, field).start()
 
     inner = pl.ds(3, planes)
-    sides = [
+    beside = [
         copy(state.at[:, :, pl.ds(rows - 3, 3)], out.at[:, inner, pl.ds(rows - 3, 3)], row_send.at[0], row_recv.at[0], along(1)),
         copy(state.at[:, :, pl.ds(0, 3)], out.at[:, inner, pl.ds(2 * rows, 3)], row_send.at[1], row_recv.at[1], along(-1)),
     ]
 
+    def trade():
+        for c in beside:
+            c.start()
+
     barrier = pltpu.get_barrier_semaphore()
-    far = slabs_x // 2
     tell(barrier, along(1))
     tell(barrier, along(-1))
 
@@ -75,39 +87,39 @@
     @pl.when(gx == 0)
     def _():
         pl.semaphore_wait(barrier, 2)
-        start(sides)
+        trade()
         pl.semaphore_wait(ready.at[0], 1)
-        start(ups)
+        cross(0)
         pl.semaphore_wait(ready.at[1], 1)
-        start(downs)
+        cross(1)
 
     @pl.when(gx == 1)
     def _():
         pl.semaphore_wait(barrier, 3)
-        start(downs)
+        cross(1)
         tell(ready.at[0], below)
-        start(sides)
+        trade()
         pl.semaphore_wait(ready.at[0], 1)
-        start(ups)
+        cross(0)
 
     @pl.when(gx == slabs_x - 1)
     def _():
         pl.semaphore_wait(barrier, 3)
-        start(ups)
+        cross(0)
         tell(ready.at[1], above)
-        start(sides)
+        trade()
         pl.semaphore_wait(ready.at[1], 1)
-        start(downs)
-
-    @pl.when(gx == far)
+        cross(1)
+
+    @pl.when(gx == slabs_x // 2)
     def _():
         pl.semaphore_wait(barrier, 4)
         tell(ready.at[0], below)
         tell(ready.at[1], above)
-        start(ups)
-        start(downs)
-        start(sides)
-
+        cross(0, 1)
+        trade()
+
+    block = pltpu.make_async_copy(state, out.at[:, inner, pl.ds(rows, rows)], own)
     block.start()
     edge = (gx == 0) | (gx == slabs_x - 1)
 
@@ -118,48 +130,94 @@
             tell(near.at[k], along(-1))
             pl.semaphore_wait(near.at[k], 2)
 
-    def forward(side, n, k, by):
-        begin, count = PARTS[n]
-        fields = pl.ds(begin, count)
-        own_rows = pl.ds(pl.multiple_of((2 + side) * rows, rows), rows)
-        their_rows = pl.ds(pl.multiple_of((2 + side - by) * rows, rows), rows)
+    def came(side, field):
+        here = slot(side, field, BASE)
+        copy(here, here, far_send.at[side], far_recv.at[side, field], along(1)).wait_recv()
+
+    def rows_of(side, field, at, start):
+        return ghost.at[side, field, :, pl.ds(at * rows + start, 3)]
+
+    def halo(side, field, k):
+        start, by = ((rows - 3, 1), (0, -1))[k]
         return copy(
-            ghost.at[side, fields, :, own_rows], ghost.at[side, fields, :, their_rows],
-            send.at[side, n, k], recv.at[side, n, k], along(by))
+            rows_of(side, field, BASE, start), rows_of(side, field, BASE - by, start),
+            halo_send.at[side, k], halo_recv.at[side, k], along(by))
+
+    def straight(side, field, k):
+        by = (2, -2)[k]
+        return copy(
+            slot(side, field, BASE), slot(side, field, BASE - by), shear_send.at[k], pass_recv.at[k, one(field)], along(by))
+
+    def to_twin(side, field, k):
+        at = (BASE, BASE - 2, BASE + 2)[k]
+        return copy(
+            slot(side, field, at), slot(side, field, at - twin), shear_send.at[2 + k], shear_recv.at[k], along(twin))
+
+    def corner(side, field, c):
+        by, start = ((-3, 0), (3, rows - 3))[c]
+        return copy(
+            rows_of(side, field, BASE, start), rows_of(side, field, BASE - by, start),
+            shear_send.at[5], shear_recv.at[3], along(by))
+
+    def haloed(field):
+        return (lax.rem(field, 3) != 2) & (field < 6)
 
     sooner = edge.astype(jnp.int32)
-    passes = ((sooner, gx == slabs_x - 1), (1 - sooner, gx == 0))
-    for side, sheared in passes:
-        for n, (begin, count) in enumerate(PARTS):
-            here = ghost.at[side, pl.ds(begin, count), :, pl.ds(pl.multiple_of((2 + side) * rows, rows), rows)]
-            copy(here, here, far_send.at[side, n], far_recv.at[side, n], along(1)).wait_recv()
-            for k, by in enumerate((1, -1)):
-                forward(side, n, k, by).start()
-
-            @pl.when(sheared)
-            def _():
-                for k, by in ((2, 2), (3, -2), (4, 6 * side - 3)):
-                    forward(side, n, k, by).start()
-    for c in ups + downs:
-        c.wait_send()
-    for c in sides:
+    for side, sheared in ((sooner, gx == slabs_x - 1), (1 - sooner, gx == 0)):
+
+        @pl.when(jnp.logical_not(sheared))
+        def _():
+            @pl.loop(0, fields)
+            def _(field):
+                came(side, field)
+
+                @pl.when(haloed(field))
+                def _():
+                    halo(side, field, 0).start()
+                    halo(side, field, 1).start()
+
+        @pl.when(sheared)
+        def _():
+            @pl.loop(0, fields)
+            def _(field):
+                came(side, field)
+                straight(side, field, 0).start()
+                straight(side, field, 1).start()
+                to_twin(side, field, 0).start()
+                for c in range(2):
+
+                    @pl.when(haloed(field) & (core == c))
+                    def _():
+                        corner(side, field, c).start()
+
+            @pl.loop(0, fields)
+            def _(field):
+                for k in range(2):
+                    straight(side, field, k).wait_recv()
+                    to_twin(side, field, 1 + k).start()
+
+            for k in range(2):
+                straight(side, every, k).wait_send()
+            for k in range(3):
+                to_twin(side, every, k).wait()
+            corner(side, pl.ds(0, HALOED), 0).wait()
+
+    for side in range(2):
+        across(side, every).wait_send()
+
+        @pl.when(gx != (slabs_x - 1) * side)
+        def _():
+            for k in range(2):
+                halo(side, pl.ds(0, HALOED), k).wait()
+
+    for c in beside:
         c.wait()
-    for side, sheared in passes:
-        for n in range(len(PARTS)):
-            for k, by in enumerate((1, -1)):
-                forward(side, n, k, by).wait()
-
-            @pl.when(sheared)
-            def _():
-                for k, by in ((2, 2), (3, -2), (4, 6 * side - 3)):
-                    forward(side, n, k, by).wait()
     block.wait()
 
 
 def extended(steps, slabs_x, slabs_y, state):
     fields, planes, rows, lanes = state.shape
-    parts = len(PARTS)
-    dma = pltpu.SemaphoreType.DMA
+    dma, plain = pltpu.SemaphoreType.DMA, pltpu.SemaphoreType.REGULAR
     return pl.pallas_call(
         functools.partial(exchange, steps, slabs_x, slabs_y),
         out_shape=(
@@ -169,10 +227,12 @@
         in_specs=[ANY],
         out_specs=(VMEM, VMEM),
         scratch_shapes=[
-            dma((2, parts, 5)), dma((2, parts, 5)), dma((2,)), dma((2,)), dma((2, parts)), dma((2, parts)), dma,
-            pltpu.SemaphoreType.REGULAR((2,)), pltpu.SemaphoreType.REGULAR((2,)),
+            dma((2,)), dma((2, fields)), dma((2,)), dma((2,)), dma((2, 2)), dma((2, 2)),
+            dma((6,)), dma((4,)), dma((2, fields)), dma, plain((2,)), plain((2,)),
         ],
-        compiler_params=pltpu.CompilerParams(collective_id=steps // SPAN, has_side_effects=True),
+        compiler_params=pltpu.CompilerParams(
+            collective_id=steps // SPAN, has_side_effects=True, vmem_limit_bytes=4 * 2**20
+        ),
         name="extended",
     )(state)
 
@@ -192,7 +252,7 @@
     left_over = lax.rem(y_shift[0] + BACK, SPAN * rows) - BACK
     by = (jnp.where(gx == 0, left_over, 0), jnp.where(gx == slabs_x - 1, -left_over, 0))
     for side in range(2):
-        start = (2 + side) * rows + by[side]
+        start = BASE * rows + by[side]
         for f in range(fields):
             for m in range(3):
                 at = side * (planes + 3) + m
@@ -217,7 +277,7 @@
     def part_near(k, x):
         return tuple([part[k, x + sign * m] for m in (1, 2, 3)] for sign in (-1, 1))
 
-    @pl.loop(0, planes + 6)
+    @pl.loop(0, planes + 6, unroll=11)
     def _(x):
         for k, f in ((0, 0), (3, 3)):
             dy = first_diff(*y_near(f + 1, x))
@@ -229,7 +289,7 @@
     inv_width = 1.0 / (slabs_x * planes)
     shear_rate = -1.5 * inv_width
 
-    @pl.loop(0, planes)
+    @pl.loop(0, planes, unroll=4)
     def _(p):
         x = p + 3
         xfrac = ((gx * planes + p).astype(jnp.float32) + 0.5) * inv_width - 0.5
@@ -312,7 +372,7 @@
         out_specs=(VMEM, VMEM, VMEM),
         input_output_aliases={2: 2},
         scratch_shapes=[pltpu.VMEM((6, planes + 6, rows, lanes), jnp.float32)],
-        compiler_params=pltpu.CompilerParams(vmem_limit_bytes=40 * 2**20),
+        compiler_params=pltpu.CompilerParams(vmem_limit_bytes=8 * 2**20),
         name="update",
     )(y_shift, ghost, ext, register, forcing)
     return new_state, new_register

time: 40.8 us -> 38.4 us (0.941)
  Pallas kernels: 38.2 us -> 35.2 us
    pallas_call x1, Pallas kernels: 5.1 us -> 2.71 us  [per_device(): pl.pallas_call(functools.partial(update, slabs_x), out_shape=(jax.ShapeDt...]
    pallas_call x1, Pallas kernels: 33.1 us -> 32.5 us  [extended(): pl.pallas_call(functools.partial(exchange, steps, slabs_x, slabs_y), out_...]
where the time goes in v3:
time: 38.4 us; the launch traced here: 38 us
  Pallas kernels  35.2 us (92%)
  between operations  1.33 us (3%)
  local copies, waits for them, and re-layouts  0.93 us (2%)
  loops' own time  0.55 us (1%)
    pallas_call x1, Pallas kernels, extended(): pl.pallas_call(functools.partial(exchange, steps, slabs_x, slabs_y), out_...  32.5 us
    pallas_call x1, Pallas kernels, per_device(): pl.pallas_call(functools.partial(update, slabs_x), out_shape=(jax.ShapeDt...  2.71 us
    unnamed x4, local copies, waits for them, and re-layouts  0.93 us

profile of v3, /device:TPU:1, one launch (start us, length us, event | category | flops | bytes accessed | tf_op | source)
XLA Modules:
  0.0 38.0 jit_solution(13163370038590085253)
XLA Ops:
  1.3 0.0 copy-start
  1.3 33.0 %conditional.1 = ((f32[7,22,24,128]{3,2,1,0:T(8,128)S(1)}, f32[2,7,3,56,128]{4,3,2,1,0:T(8,128)S(1)})) conditional(s32[]{:T(128)} %clamp.3, f32[7,16,8,128]{3,2,1,0:T(8,128)} %param.36, f32[7,16,8,128]{3,2,1,0:T(8,128)} %param.36, f32[7,16,8,128]{3,2,1,0:T(8,128)} %param.36, f32[7,16,8,128]{3,2,1,0:T(8,128)} %param.36, ...), branch_computations={%region_0.0_spmd, %region_1.0_spmd, %region_2.0_spmd, %region_3.0_... | conditional | bytes 8 | solution.py:361
  1.6 32.5 %extended.60 = (f32[7,22,24,128]{3,2,1,0:T(8,128)S(1)}, f32[2,7,3,56,128]{4,3,2,1,0:T(8,128)S(1)}) custom-call(f32[7,16,8,128]{3,2,1,0:T(8,128)} %state.28), custom_call_target="tpu_custom_call" | custom-call | tf_op jit(solution)/shard_map/cond/branch_28_fun/extended/pallas_call | solution.py:221
  34.3 0.0 copy-done
  34.3 0.0 copy-start.1
  34.3 0.9 %copy-done.1 = f32[3,16,8,128]{3,2,1,0:T(8,128)S(1)} copy-done((f32[3,16,8,128]{3,2,1,0:T(8,128)S(1)}, f32[3,16,8,128]{3,2,1,0:T(8,128)}, u32[]{:S(2)}) %copy-start.1) | copy-done | bytes 196632
  35.3 2.7 %update.1 = (f32[7,16,8,128]{3,2,1,0:T(8,128)}, f32[7,16,8,128]{3,2,1,0:T(8,128)}, f32[7,22,24,128]{3,2,1,0:T(8,128)S(1)}) custom-call(s32[1]{0:T(128)S(6)} %copy.72.y_shift, f32[2,7,3,56,128]{4,3,2,1,0:T(8,128)S(1)} %get-tuple-element.38.ghost, f32[7,22,24,128]{3,2,1,0:T(8,128)S(1)} %get-tuple-element.39.ext_in, ...), custom_call_target="tpu_custom_call", output_to_operand_aliasing={{2}: (2, {})} | custom-call | tf_op jit(solution)/shard_map/update/pallas_call | solution.py:368
Async XLA Ops:
  1.3 33.0 %copy-start = (f32[7,16,8,128]{3,2,1,0:T(8,128)S(1)}, f32[7,16,8,128]{3,2,1,0:T(8,128)}, u32[]{:S(2)}) copy-start(f32[7,16,8,128]{3,2,1,0:T(8,128)} %register.1) | copy-start | bytes 1376260
  34.3 0.9 %copy-start.1 = (f32[3,16,8,128]{3,2,1,0:T(8,128)S(1)}, f32[3,16,8,128]{3,2,1,0:T(8,128)}, u32[]{:S(2)}) copy-start(f32[3,16,8,128]{3,2,1,0:T(8,128)} %forcing.1) | copy-start | bytes 589828

commit v4 on v3

--- a/solution.py
+++ b/solution.py
@@ -21,7 +21,7 @@
 
 def exchange(
     steps, slabs_x, slabs_y, state, out, ghost, far_send, far_recv, row_send, row_recv, halo_send, halo_recv,
-    shear_send, shear_recv, pass_recv, own, ready, near
+    shear_send, shear_recv, pass_recv, twice_send, own, ready, near
 ):
     gx = lax.axis_index("gx")
     yz = lax.axis_index("yz")
@@ -64,14 +64,26 @@
 
     inner = pl.ds(3, planes)
     beside = [
-        copy(state.at[:, :, pl.ds(rows - 3, 3)], out.at[:, inner, pl.ds(rows - 3, 3)], row_send.at[0], row_recv.at[0], along(1)),
-        copy(state.at[:, :, pl.ds(0, 3)], out.at[:, inner, pl.ds(2 * rows, 3)], row_send.at[1], row_recv.at[1], along(-1)),
+        copy(state.at[:, :, pl.ds(rows - 3, 3)], out.at[:, inner, pl.ds(0, 3)], row_send.at[0], row_recv.at[0], along(1)),
+        copy(state.at[:, :, pl.ds(0, 3)], out.at[:, inner, pl.ds(rows + 3, 3)], row_send.at[1], row_recv.at[1], along(-1)),
     ]
 
     def trade():
         for c in beside:
             c.start()
 
+    ahead = lax.rem(yz + (slabs_y - steps), slabs_y)
+    doubled = (gx == slabs_x - 1) & ((ahead < 2) | (ahead >= slabs_y - 2))
+    spared = ((gx == 0) & (yz >= slabs_y - 2), (gx == 0) & (yz < 2))
+    served = spared[0] | spared[1]
+
+    def twice(field):
+        downward = (ahead < 2).astype(jnp.int32)
+        by = 2 - 4 * downward
+        source = state.at[field, pl.ds(planes - 3, 3)]
+        peer = {"yz": lax.rem(ahead + (slabs_y + by), slabs_y), "gx": lax.rem(gx + 1, slabs_x)}
+        return copy(source, slot(0, field, BASE - by), twice_send, pass_recv.at[downward, one(field)], peer)
+
     barrier = pltpu.get_barrier_semaphore()
     tell(barrier, along(1))
     tell(barrier, along(-1))
@@ -83,6 +95,11 @@
     @pl.when((gx == 0) | (gx == slabs_x - 1))
     def _():
         tell(barrier, below)
+
+    @pl.when(served)
+    def _():
+        over = 2 - 4 * (yz < 2).astype(jnp.int32)
+        tell(barrier, {"yz": lax.rem(yz + (slabs_y + steps) + over, slabs_y), "gx": lax.rem(gx + slabs_x - 1, slabs_x)})
 
     @pl.when(gx == 0)
     def _():
@@ -104,9 +121,16 @@
 
     @pl.when(gx == slabs_x - 1)
     def _():
-        pl.semaphore_wait(barrier, 3)
+        pl.semaphore_wait(barrier, 3 + doubled.astype(jnp.int32))
         cross(0)
         tell(ready.at[1], above)
+
+        @pl.when(doubled)
+        def _():
+            @pl.loop(0, fields)
+            def _(field):
+                twice(field).start()
+
         trade()
         pl.semaphore_wait(ready.at[1], 1)
         cross(1)
@@ -119,7 +143,7 @@
         cross(0, 1)
         trade()
 
-    block = pltpu.make_async_copy(state, out.at[:, inner, pl.ds(rows, rows)], own)
+    block = pltpu.make_async_copy(state, out.at[:, inner, pl.ds(3, rows)], own)
     block.start()
     edge = (gx == 0) | (gx == slabs_x - 1)
 
@@ -162,45 +186,58 @@
     def haloed(field):
         return (lax.rem(field, 3) != 2) & (field < 6)
 
-    sooner = edge.astype(jnp.int32)
-    for side, sheared in ((sooner, gx == slabs_x - 1), (1 - sooner, gx == 0)):
-
-        @pl.when(jnp.logical_not(sheared))
-        def _():
-            @pl.loop(0, fields)
-            def _(field):
-                came(side, field)
-
-                @pl.when(haloed(field))
+    def halos(side):
+        @pl.loop(0, fields)
+        def _(field):
+            came(side, field)
+
+            @pl.when(haloed(field))
+            def _():
+                halo(side, field, 0).start()
+                halo(side, field, 1).start()
+
+    def sheared(side):
+        @pl.loop(0, fields)
+        def _(field):
+            came(side, field)
+            to_twin(side, field, 0).start()
+            for k in range(2):
+
+                @pl.when(jnp.logical_not(spared[k]))
                 def _():
-                    halo(side, field, 0).start()
-                    halo(side, field, 1).start()
-
-        @pl.when(sheared)
-        def _():
-            @pl.loop(0, fields)
-            def _(field):
-                came(side, field)
-                straight(side, field, 0).start()
-                straight(side, field, 1).start()
-                to_twin(side, field, 0).start()
-                for c in range(2):
-
-                    @pl.when(haloed(field) & (core == c))
-                    def _():
-                        corner(side, field, c).start()
-
-            @pl.loop(0, fields)
-            def _(field):
-                for k in range(2):
-                    straight(side, field, k).wait_recv()
-                    to_twin(side, field, 1 + k).start()
-
+                    straight(side, field, k).start()
+
+            for c in range(2):
+
+                @pl.when(haloed(field) & (core == c))
+                def _():
+                    corner(side, field, c).start()
+
+        @pl.loop(0, fields)
+        def _(field):
             for k in range(2):
+                straight(side, field, k).wait_recv()
+                to_twin(side, field, 1 + k).start()
+
+        for k in range(2):
+
+            @pl.when(jnp.logical_not(spared[k]))
+            def _():
                 straight(side, every, k).wait_send()
-            for k in range(3):
-                to_twin(side, every, k).wait()
-            corner(side, pl.ds(0, HALOED), 0).wait()
+
+        for k in range(3):
+            to_twin(side, every, k).wait()
+        corner(side, pl.ds(0, HALOED), 0).wait()
+
+    halos(first)
+
+    @pl.when(jnp.logical_not(edge))
+    def _():
+        halos(1 - first)
+
+    @pl.when(edge)
+    def _():
+        sheared(1 - first)
 
     for side in range(2):
         across(side, every).wait_send()
@@ -209,6 +246,10 @@
         def _():
             for k in range(2):
                 halo(side, pl.ds(0, HALOED), k).wait()
+
+    @pl.when(doubled)
+    def _():
+        twice(every).wait_send()
 
     for c in beside:
         c.wait()
@@ -221,14 +262,14 @@
     return pl.pallas_call(
         functools.partial(exchange, steps, slabs_x, slabs_y),
         out_shape=(
-            pltpu.VMEM((fields, planes + 6, 3 * rows, lanes), state.dtype),
+            pltpu.VMEM((fields, planes + 6, 2 * rows, lanes), state.dtype),
             pltpu.VMEM((2, fields, 3, SLOTS * rows, lanes), state.dtype),
         ),
         in_specs=[ANY],
         out_specs=(VMEM, VMEM),
         scratch_shapes=[
             dma((2,)), dma((2, fields)), dma((2,)), dma((2,)), dma((2, 2)), dma((2, 2)),
-            dma((6,)), dma((4,)), dma((2, fields)), dma, plain((2,)), plain((2,)),
+            dma((6,)), dma((4,)), dma((2, fields)), dma, dma, plain((2,)), plain((2,)),
         ],
         compiler_params=pltpu.CompilerParams(
             collective_id=steps // SPAN, has_side_effects=True, vmem_limit_bytes=4 * 2**20
@@ -256,14 +297,14 @@
         for f in range(fields):
             for m in range(3):
                 at = side * (planes + 3) + m
-                ext[f, at, pl.ds(rows - 3, rows)] = ghost[side, f, m, pl.ds(start - 3, rows)]
-                ext[f, at, pl.ds(rows + 3, rows)] = ghost[side, f, m, pl.ds(start + 3, rows)]
+                ext[f, at, pl.ds(0, rows)] = ghost[side, f, m, pl.ds(start - 3, rows)]
+                ext[f, at, pl.ds(rows, rows)] = ghost[side, f, m, pl.ds(start + rows - 3, rows)]
 
     def y_near(f, x):
-        return tuple([ext[f, x, pl.ds(rows + sign * k, rows)] for k in (1, 2, 3)] for sign in (-1, 1))
+        return tuple([ext[f, x, pl.ds(3 + sign * k, rows)] for k in (1, 2, 3)] for sign in (-1, 1))
 
     def x_near(f, x):
-        return tuple([ext[f, x + sign * k, pl.ds(rows, rows)] for k in (1, 2, 3)] for sign in (-1, 1))
+        return tuple([ext[f, x + sign * k, pl.ds(3, rows)] for k in (1, 2, 3)] for sign in (-1, 1))
 
     def z_near(value):
         return (
@@ -272,7 +313,7 @@
         )
 
     def center(f, x):
-        return ext[f, x, pl.ds(rows, rows)]
+        return ext[f, x, pl.ds(3, rows)]
 
     def part_near(k, x):
         return tuple([part[k, x + sign * m] for m in (1, 2, 3)] for sign in (-1, 1))

time: 38.4 us -> 35.2 us (0.917)
  the two profiles are of different devices: /device:TPU:1 before, /device:TPU:8 now
where the time goes in v4:
time: 35.2 us; the launch traced here: 35 us
  Pallas kernels  33.4 us (95%)
  between operations  1.34 us (4%)
    pallas_call x1, Pallas kernels, extended(): pl.pallas_call(functools.partial(exchange, steps, slabs_x, slabs_y), out_...  30.6 us
    pallas_call x1, Pallas kernels, per_device(): pl.pallas_call(functools.partial(update, slabs_x), out_shape=(jax.ShapeDt...  2.82 us

profile of v4, /device:TPU:8, one launch (start us, length us, event | category | flops | bytes accessed | tf_op | source)
XLA Modules:
  0.0 35.0 jit_solution(12108146167911409359)
XLA Ops:
  1.3 0.0 copy-start
  1.3 0.0 copy-start.1
  1.3 30.9 %conditional.1 = ((f32[7,22,16,128]{3,2,1,0:T(8,128)S(1)}, f32[2,7,3,56,128]{4,3,2,1,0:T(8,128)S(1)})) conditional(s32[]{:T(128)} %clamp.3, f32[7,16,8,128]{3,2,1,0:T(8,128)} %param.36, f32[7,16,8,128]{3,2,1,0:T(8,128)} %param.36, f32[7,16,8,128]{3,2,1,0:T(8,128)} %param.36, f32[7,16,8,128]{3,2,1,0:T(8,128)} %param.36, ...), branch_computations={%region_0.0_spmd, %region_1.0_spmd, %region_2.0_spmd, %region_3.0_... | conditional | bytes 8 | solution.py:402
  1.4 30.6 %extended.41 = (f32[7,22,16,128]{3,2,1,0:T(8,128)S(1)}, f32[2,7,3,56,128]{4,3,2,1,0:T(8,128)S(1)}) custom-call(f32[7,16,8,128]{3,2,1,0:T(8,128)} %state.9), custom_call_target="tpu_custom_call" | custom-call | tf_op jit(solution)/shard_map/cond/branch_9_fun/extended/pallas_call | solution.py:262
  32.2 0.0 copy-done
  32.2 0.0 copy-done.1
  32.2 2.8 %update.1 = (f32[7,16,8,128]{3,2,1,0:T(8,128)}, f32[7,16,8,128]{3,2,1,0:T(8,128)}, f32[7,22,16,128]{3,2,1,0:T(8,128)S(1)}) custom-call(s32[1]{0:T(128)S(6)} %copy.72.y_shift, f32[2,7,3,56,128]{4,3,2,1,0:T(8,128)S(1)} %get-tuple-element.38.ghost, f32[7,22,16,128]{3,2,1,0:T(8,128)S(1)} %get-tuple-element.39.ext_in, ...), custom_call_target="tpu_custom_call", output_to_operand_aliasing={{2}: (2, {})} | custom-call | tf_op jit(solution)/shard_map/update/pallas_call | solution.py:409
Async XLA Ops:
  1.3 30.9 %copy-start = (f32[7,16,8,128]{3,2,1,0:T(8,128)S(1)}, f32[7,16,8,128]{3,2,1,0:T(8,128)}, u32[]{:S(2)}) copy-start(f32[7,16,8,128]{3,2,1,0:T(8,128)} %register.1) | copy-start | bytes 1376260
  1.3 30.9 %copy-start.1 = (f32[3,16,8,128]{3,2,1,0:T(8,128)S(1)}, f32[3,16,8,128]{3,2,1,0:T(8,128)}, u32[]{:S(2)}) copy-start(f32[3,16,8,128]{3,2,1,0:T(8,128)} %forcing.1) | copy-start | bytes 589828

commit v5 on v4

--- a/solution.py
+++ b/solution.py
@@ -84,6 +84,10 @@
         peer = {"yz": lax.rem(ahead + (slabs_y + by), slabs_y), "gx": lax.rem(gx + 1, slabs_x)}
         return copy(source, slot(0, field, BASE - by), twice_send, pass_recv.at[downward, one(field)], peer)
 
+    def hail(k):
+        tell(near.at[k], along(1))
+        tell(near.at[k], along(-1))
+
     barrier = pltpu.get_barrier_semaphore()
     tell(barrier, along(1))
     tell(barrier, along(-1))
@@ -104,9 +108,12 @@
     @pl.when(gx == 0)
     def _():
         pl.semaphore_wait(barrier, 2)
+        hail(0)
         trade()
         pl.semaphore_wait(ready.at[0], 1)
         cross(0)
+        pl.semaphore_wait(near.at[0], 2)
+        hail(1)
         pl.semaphore_wait(ready.at[1], 1)
         cross(1)
 
@@ -131,7 +138,10 @@
             def _(field):
                 twice(field).start()
 
+        hail(0)
         trade()
+        pl.semaphore_wait(near.at[0], 2)
+        hail(1)
         pl.semaphore_wait(ready.at[1], 1)
         cross(1)
 
@@ -149,10 +159,7 @@
 
     @pl.when(edge)
     def _():
-        for k in range(2):
-            tell(near.at[k], along(1))
-            tell(near.at[k], along(-1))
-            pl.semaphore_wait(near.at[k], 2)
+        pl.semaphore_wait(near.at[1], 2)
 
     def came(side, field):
         here = slot(side, field, BASE)

time: 35.2 us -> 33.5 us (0.952)
  the two profiles are of different devices: /device:TPU:8 before, /device:TPU:65 now
where the time goes in v5:
time: 33.5 us
  Pallas kernels  31.8 us (95%)
  between operations  1.34 us (4%)
    pallas_call x1, Pallas kernels, extended(): pl.pallas_call(functools.partial(exchange, steps, slabs_x, slabs_y), out_...  29 us
    pallas_call x1, Pallas kernels, per_device(): pl.pallas_call(functools.partial(update, slabs_x), out_shape=(jax.ShapeDt...  2.82 us

profile of v5, /device:TPU:65, one launch (start us, length us, event | category | flops | bytes accessed | tf_op | source)
XLA Modules:
  0.0 33.5 jit_solution(17107359280003089371)
XLA Ops:
  1.3 0.0 copy-start
  1.3 0.0 copy-start.1
  1.3 29.3 %conditional.1 = ((f32[7,22,16,128]{3,2,1,0:T(8,128)S(1)}, f32[2,7,3,56,128]{4,3,2,1,0:T(8,128)S(1)})) conditional(s32[]{:T(128)} %clamp.3, f32[7,16,8,128]{3,2,1,0:T(8,128)} %param.36, f32[7,16,8,128]{3,2,1,0:T(8,128)} %param.36, f32[7,16,8,128]{3,2,1,0:T(8,128)} %param.36, f32[7,16,8,128]{3,2,1,0:T(8,128)} %param.36, ...), branch_computations={%region_0.0_spmd, %region_1.0_spmd, %region_2.0_spmd, %region_3.0_... | conditional | bytes 8 | solution.py:409
  1.4 29.0 %extended.42 = (f32[7,22,16,128]{3,2,1,0:T(8,128)S(1)}, f32[2,7,3,56,128]{4,3,2,1,0:T(8,128)S(1)}) custom-call(f32[7,16,8,128]{3,2,1,0:T(8,128)} %state.10), custom_call_target="tpu_custom_call" | custom-call | tf_op jit(solution)/shard_map/cond/branch_10_fun/extended/pallas_call | solution.py:269
  30.6 0.0 copy-done
  30.6 0.0 copy-done.1
  30.7 2.8 %update.1 = (f32[7,16,8,128]{3,2,1,0:T(8,128)}, f32[7,16,8,128]{3,2,1,0:T(8,128)}, f32[7,22,16,128]{3,2,1,0:T(8,128)S(1)}) custom-call(s32[1]{0:T(128)S(6)} %copy.72.y_shift, f32[2,7,3,56,128]{4,3,2,1,0:T(8,128)S(1)} %get-tuple-element.38.ghost, f32[7,22,16,128]{3,2,1,0:T(8,128)S(1)} %get-tuple-element.39.ext_in, ...), custom_call_target="tpu_custom_call", output_to_operand_aliasing={{2}: (2, {})} | custom-call | tf_op jit(solution)/shard_map/update/pallas_call | solution.py:416
Async XLA Ops:
  1.3 29.3 %copy-start = (f32[7,16,8,128]{3,2,1,0:T(8,128)S(1)}, f32[7,16,8,128]{3,2,1,0:T(8,128)}, u32[]{:S(2)}) copy-start(f32[7,16,8,128]{3,2,1,0:T(8,128)} %register.1) | copy-start | bytes 1376260
  1.3 29.3 %copy-start.1 = (f32[3,16,8,128]{3,2,1,0:T(8,128)S(1)}, f32[3,16,8,128]{3,2,1,0:T(8,128)}, u32[]{:S(2)}) copy-start(f32[3,16,8,128]{3,2,1,0:T(8,128)} %forcing.1) | copy-start | bytes 589828
